TPU v7x, 128 devices: a whole 4x4x4 slice. The times are simulated.
128 devices in a mesh: depth: 8 (over z, core), row: 16 (over y, x).
Axes of the slice: x: 4, y: 4, z: 4, core: 2. Of those that a mesh axis runs over, the one named last changes fastest.
Arguments:
- volume: float32 [384, 1024, 2048], P('depth', 'row'), may hold values from -6 to 6
- transfer: float32 [8], replicated, may hold values from 0.3 to 1.2
Outputs:
- image: float32 [4, 1024, 2048], P(None, 'row', 'depth')
All inputs are finite; a program needn't handle non-finite values.
Results may differ from a plain program's by a relative error of at most 0.0003.
Values sent between devices are 32-bit elements; how exact they have to be, the bound alone decides.
A program may use at most 192 MiB of HBM per device.

v0:
```python
import jax
import jax.numpy as jnp
from jax import lax
from jax.sharding import PartitionSpec as P


def with_halo(cells, sides, width):
    for axis, dim in sides:
        count = lax.axis_size(axis)
        ends = count - 1
        head = lax.slice_in_dim(cells, 0, width, axis=dim)
        tail = lax.slice_in_dim(cells, cells.shape[dim] - width, cells.shape[dim], axis=dim)
        cells = jnp.concatenate(
            [
                lax.ppermute(tail, axis, [(i, (i + 1) % count) for i in range(ends)]),
                cells,
                lax.ppermute(head, axis, [((i + 1) % count, i) for i in range(ends)]),
            ],
            axis=dim,
        )
    return cells


def slope_cols(center):
    zero_col = jnp.zeros_like(center[..., :1])
    right = jnp.concatenate([center[..., 1:], zero_col], -1)
    left = jnp.concatenate([zero_col, center[..., :-1]], -1)
    return 0.5 * (right - left)


def emit(framed, transfer, slices):
    center = framed[1:-1, 1:-1, :]
    slope_depth = 0.5 * (framed[2:, 1:-1, :] - framed[:-2, 1:-1, :])
    slope_row = 0.5 * (framed[1:-1, 2:, :] - framed[1:-1, :-2, :])
    slope_col = slope_cols(center)
    inverse = lax.rsqrt(
        slope_depth * slope_depth + slope_row * slope_row + slope_col * slope_col + 1.0
    )
    lambert = jnp.abs((slope_depth + 2.0 * slope_row + 2.0 * slope_col) * inverse) / 3.0
    ambient = 0.5 * transfer[7]
    shading = ambient + (1.0 - ambient) * lambert
    depth_term = 2.0 * transfer[6] / slices * jax.nn.softplus(center)
    opacity = -jnp.expm1(-depth_term)
    tinting = jax.nn.sigmoid(2.0 * center)
    weight = shading * opacity
    emitted = jnp.stack(
        [(transfer[channel] + transfer[3 + channel] * tinting) * weight for channel in range(3)]
    )
    return (emitted, depth_term)


def blend_parts(parts):
    depth_parts = parts[:, 3]
    before = jnp.cumsum(depth_parts, 0) - depth_parts
    color = jnp.sum(jnp.exp(-before)[:, None] * parts[:, :3], 0)
    total = jnp.sum(depth_parts, 0)
    return jnp.concatenate([color, total[None]], 0)


def on_device(volume, transfer):
    local_slices, local_rows, columns = volume.shape
    groups = lax.axis_size("depth")
    slices = local_slices * groups
    padded = with_halo(volume, (("depth", 0), ("row", 1)), 1)
    steps = local_slices // 8

    def march(carry, index):
        color, depth_acc = carry
        slab = lax.dynamic_slice_in_dim(padded, index * 8, 10, 0)
        emitted, depth_term = emit(slab, transfer, slices)
        before = jnp.cumsum(depth_term, 0) - depth_term
        passing = jnp.exp(-(depth_acc[None] + before))
        color = color + jnp.sum(passing[None] * emitted, 1)
        depth_acc = depth_acc + jnp.sum(depth_term, 0)
        return ((color, depth_acc), None)

    start_color = jnp.zeros((3, local_rows, columns), jnp.float32)
    start_depth = jnp.zeros((local_rows, columns), jnp.float32)
    (color, depth_acc), unused = lax.scan(
        march, (start_color, start_depth), jnp.arange(steps, dtype=jnp.int32)
    )
    partial_image = jnp.concatenate([color, depth_acc[None]], 0)
    final = blend_parts(
        lax.all_to_all(partial_image[None], "depth", split_axis=3, concat_axis=0, tiled=True)
    )
    return jnp.concatenate([final[:3], -jnp.expm1(-final[3:4])], 0)


def solution(mesh):
    in_specs = (P("depth", "row", None), P())
    out_specs = P(None, "row", "depth")
    return jax.shard_map(
        on_device, mesh=mesh, in_specs=in_specs, out_specs=out_specs, check_vma=False
    )
```

profile of v0, /device:TPU:14, one launch (start us, length us, event | category | flops | bytes accessed | tf_op | source)
XLA Modules:
  0.0 483.0 jit_solution(13706453914436330940)
XLA Ops:
  4.6 10.6 %constant_dynamic-update-slice_fusion.1 = f32[50,64,2048]{2,1,0:T(8,128)S(1)} fusion(f32[50,64,2048]{2,1,0:T(8,128)S(1)} %constant_dynamic-update-slice_fusion.2, f32[48,64,2048]{2,1,0:T(8,128)} %param.4), kind=kLoop, calls=%fused_computation.28 | loop fusion | bytes 50331648
  28.7 7.4 %collective-permute-done.3 = f32[50,1,2048]{2,1,0:T(1,128)} collective-permute-done((f32[50,1,2048]{2,1,0:T(1,128)S(1)}, f32[50,1,2048]{2,1,0:T(1,128)}, u32[]{:S(2)}, u32[]{:S(2)}) %collective-permute-start.3) | collective-permute-done | bytes 409632 | tf_op jit(solution)/shard_map/ppermute | solution.py:17
  36.0 20.7 %pad_maximum_fusion = f32[50,66,2048]{2,1,0:T(8,128)} fusion(f32[50,1,2048]{2,1,0:T(1,128)} %collective-permute-done.3, f32[50,64,2048]{2,1,0:T(8,128)} %copy-done.2, f32[50,1,2048]{2,1,0:T(1,128)S(1)} %collective-permute-done.2), kind=kLoop, calls=%fused_computation.17 | loop fusion | flops 13516800 | bytes 54067200 | tf_op jit(solution)/shard_map/concatenate | solution.py:13
  56.7 343.4 %while.16 = (s32[]{:T(128)}, f32[3,64,2048]{2,1,0:T(8,128)S(1)}, f32[64,2048]{1,0:T(8,128)S(1)}, f32[]{:T(128)}, s32[6]{0:T(128)S(1)}, /*index=5*/f32[50,66,2048...) while((s32[]{:T(128)}, f32[3,64,2048]{2,1,0:T(8,128)S(1)}, ...), condition=%wide.region_4.5_spmd.clone, body=%wide.region_0.4_spmd.clone.sunk | while | flops 86507528 | bytes 139449296 | solution.py:79
  57.8 8.3 %fusion.22 = (f32[8,64,2047]{2,1,0:T(8,128)}, f32[8,64,2047]{2,1,0:T(8,128)}) fusion(f32[50,66,2048]{2,1,0:T(8,128)} %get-tuple-element.322, s32[]{:T(128)S(6)} %add.257, s32[]{:T(128)S(6)} %add.258), kind=kLoop, calls=%fused_computation.31.clone.1 | loop fusion | bytes 16769032 | tf_op jit(solution)/shard_map/while/body/eval_jaxpr/slice | solution.py:26
  66.7 18.1 %multiply_bitcast_fusion.5 = (f32[1,8,64,2048]{3,2,1,0:T(8,128)}, f32[8,64,2048]{2,1,0:T(8,128)S(1)}) fusion(f32[]{:T(128)} %bitcast.41, f32[]{:T(128)} %bitcast.42, f32[50,66,2048]{2,1,0:T(8,128)} %get-tuple-element.322, s32[]{:T(128)S(6)} %add.257, s32[]{:T(128)S(6)} %add.258, f32[]{:T(128)} %get-tuple-element.320, f32[]{:T(128)} %get-tuple-element.325, ...), kind=kLoop, calls=%fused_computation.9.clone.1 | loop fusion | flops 36700160 | bytes 37744680 | tf_op jit(solution)/shard_map/while/body/eval_jaxpr/stack | solution.py:46
  84.9 10.4 %multiply_bitcast_fusion.6 = (f32[1,8,64,2048]{3,2,1,0:T(8,128)}, f32[1,8,64,2048]{3,2,1,0:T(8,128)}, f32[64,2048]{1,0:T(8,128)S(1)}) fusion(f32[8,64,2048]{2,1,0:T(8,128)S(1)} %get-tuple-element.276, f32[]{:T(128)} %bitcast.44, f32[]{:T(128)} %bitcast.45, f32[50,66,2048]{2,1,0:T(8,128)} %get-tuple-element.322, s32[]{:T(128)S(6)} %add.257, ...), kind=kLoop, calls=%fused_computation.8.clone.1 | loop fusion | flops 18743296 | bytes 17301532 | tf_op jit(solution)/shard_map/while/body/eval_jaxpr/stack | solution.py:46
  95.5 12.9 %negate_exponential_fusion.3 = f32[8,64,2048]{2,1,0:T(8,128)S(1)} fusion(f32[64,2048]{1,0:T(8,128)S(1)} %get-tuple-element.285, f32[50,66,2048]{2,1,0:T(8,128)} %get-tuple-element.322, s32[]{:T(128)S(6)} %add.257, s32[]{:T(128)S(6)} %add.258, f32[]{:T(128)} %get-tuple-element.320), kind=kOutput, calls=%fused_computation.12.clone.1 | output fusion | flops 17825792 | bytes 8913416 | tf_op jit(solution)/shard_map/while/body/eval_jaxpr/jit(cumsum)/reduce_window_sum | solution.py:71
  114.1 8.3 %fusion.22 = (f32[8,64,2047]{2,1,0:T(8,128)}, f32[8,64,2047]{2,1,0:T(8,128)}) fusion(f32[50,66,2048]{2,1,0:T(8,128)} %get-tuple-element.322, s32[]{:T(128)S(6)} %add.257, s32[]{:T(128)S(6)} %add.258), kind=kLoop, calls=%fused_computation.31.clone.1 | loop fusion | bytes 16769032 | tf_op jit(solution)/shard_map/while/body/eval_jaxpr/slice | solution.py:26
  123.0 18.2 %multiply_bitcast_fusion.5 = (f32[1,8,64,2048]{3,2,1,0:T(8,128)}, f32[8,64,2048]{2,1,0:T(8,128)S(1)}) fusion(f32[]{:T(128)} %bitcast.41, f32[]{:T(128)} %bitcast.42, f32[50,66,2048]{2,1,0:T(8,128)} %get-tuple-element.322, s32[]{:T(128)S(6)} %add.257, s32[]{:T(128)S(6)} %add.258, f32[]{:T(128)} %get-tuple-element.320, f32[]{:T(128)} %get-tuple-element.325, ...), kind=kLoop, calls=%fused_computation.9.clone.1 | loop fusion | flops 36700160 | bytes 37744680 | tf_op jit(solution)/shard_map/while/body/eval_jaxpr/stack | solution.py:46
  141.2 10.4 %multiply_bitcast_fusion.6 = (f32[1,8,64,2048]{3,2,1,0:T(8,128)}, f32[1,8,64,2048]{3,2,1,0:T(8,128)}, f32[64,2048]{1,0:T(8,128)S(1)}) fusion(f32[8,64,2048]{2,1,0:T(8,128)S(1)} %get-tuple-element.276, f32[]{:T(128)} %bitcast.44, f32[]{:T(128)} %bitcast.45, f32[50,66,2048]{2,1,0:T(8,128)} %get-tuple-element.322, s32[]{:T(128)S(6)} %add.257, ...), kind=kLoop, calls=%fused_computation.8.clone.1 | loop fusion | flops 18743296 | bytes 17301532 | tf_op jit(solution)/shard_map/while/body/eval_jaxpr/stack | solution.py:46
  151.9 14.1 %negate_exponential_fusion.3 = f32[8,64,2048]{2,1,0:T(8,128)S(1)} fusion(f32[64,2048]{1,0:T(8,128)S(1)} %get-tuple-element.285, f32[50,66,2048]{2,1,0:T(8,128)} %get-tuple-element.322, s32[]{:T(128)S(6)} %add.257, s32[]{:T(128)S(6)} %add.258, f32[]{:T(128)} %get-tuple-element.320), kind=kOutput, calls=%fused_computation.12.clone.1 | output fusion | flops 17825792 | bytes 8913416 | tf_op jit(solution)/shard_map/while/body/eval_jaxpr/jit(cumsum)/reduce_window_sum | solution.py:71
  171.6 8.3 %fusion.22 = (f32[8,64,2047]{2,1,0:T(8,128)}, f32[8,64,2047]{2,1,0:T(8,128)}) fusion(f32[50,66,2048]{2,1,0:T(8,128)} %get-tuple-element.322, s32[]{:T(128)S(6)} %add.257, s32[]{:T(128)S(6)} %add.258), kind=kLoop, calls=%fused_computation.31.clone.1 | loop fusion | bytes 16769032 | tf_op jit(solution)/shard_map/while/body/eval_jaxpr/slice | solution.py:26
  180.6 18.1 %multiply_bitcast_fusion.5 = (f32[1,8,64,2048]{3,2,1,0:T(8,128)}, f32[8,64,2048]{2,1,0:T(8,128)S(1)}) fusion(f32[]{:T(128)} %bitcast.41, f32[]{:T(128)} %bitcast.42, f32[50,66,2048]{2,1,0:T(8,128)} %get-tuple-element.322, s32[]{:T(128)S(6)} %add.257, s32[]{:T(128)S(6)} %add.258, f32[]{:T(128)} %get-tuple-element.320, f32[]{:T(128)} %get-tuple-element.325, ...), kind=kLoop, calls=%fused_computation.9.clone.1 | loop fusion | flops 36700160 | bytes 37744680 | tf_op jit(solution)/shard_map/while/body/eval_jaxpr/stack | solution.py:46
  198.7 10.4 %multiply_bitcast_fusion.6 = (f32[1,8,64,2048]{3,2,1,0:T(8,128)}, f32[1,8,64,2048]{3,2,1,0:T(8,128)}, f32[64,2048]{1,0:T(8,128)S(1)}) fusion(f32[8,64,2048]{2,1,0:T(8,128)S(1)} %get-tuple-element.276, f32[]{:T(128)} %bitcast.44, f32[]{:T(128)} %bitcast.45, f32[50,66,2048]{2,1,0:T(8,128)} %get-tuple-element.322, s32[]{:T(128)S(6)} %add.257, ...), kind=kLoop, calls=%fused_computation.8.clone.1 | loop fusion | flops 18743296 | bytes 17301532 | tf_op jit(solution)/shard_map/while/body/eval_jaxpr/stack | solution.py:46
  209.3 14.2 %negate_exponential_fusion.3 = f32[8,64,2048]{2,1,0:T(8,128)S(1)} fusion(f32[64,2048]{1,0:T(8,128)S(1)} %get-tuple-element.285, f32[50,66,2048]{2,1,0:T(8,128)} %get-tuple-element.322, s32[]{:T(128)S(6)} %add.257, s32[]{:T(128)S(6)} %add.258, f32[]{:T(128)} %get-tuple-element.320), kind=kOutput, calls=%fused_computation.12.clone.1 | output fusion | flops 17825792 | bytes 8913416 | tf_op jit(solution)/shard_map/while/body/eval_jaxpr/jit(cumsum)/reduce_window_sum | solution.py:71
  229.1 8.3 %fusion.22 = (f32[8,64,2047]{2,1,0:T(8,128)}, f32[8,64,2047]{2,1,0:T(8,128)}) fusion(f32[50,66,2048]{2,1,0:T(8,128)} %get-tuple-element.322, s32[]{:T(128)S(6)} %add.257, s32[]{:T(128)S(6)} %add.258), kind=kLoop, calls=%fused_computation.31.clone.1 | loop fusion | bytes 16769032 | tf_op jit(solution)/shard_map/while/body/eval_jaxpr/slice | solution.py:26
  238.1 17.9 %multiply_bitcast_fusion.5 = (f32[1,8,64,2048]{3,2,1,0:T(8,128)}, f32[8,64,2048]{2,1,0:T(8,128)S(1)}) fusion(f32[]{:T(128)} %bitcast.41, f32[]{:T(128)} %bitcast.42, f32[50,66,2048]{2,1,0:T(8,128)} %get-tuple-element.322, s32[]{:T(128)S(6)} %add.257, s32[]{:T(128)S(6)} %add.258, f32[]{:T(128)} %get-tuple-element.320, f32[]{:T(128)} %get-tuple-element.325, ...), kind=kLoop, calls=%fused_computation.9.clone.1 | loop fusion | flops 36700160 | bytes 37744680 | tf_op jit(solution)/shard_map/while/body/eval_jaxpr/stack | solution.py:46
  256.0 10.4 %multiply_bitcast_fusion.6 = (f32[1,8,64,2048]{3,2,1,0:T(8,128)}, f32[1,8,64,2048]{3,2,1,0:T(8,128)}, f32[64,2048]{1,0:T(8,128)S(1)}) fusion(f32[8,64,2048]{2,1,0:T(8,128)S(1)} %get-tuple-element.276, f32[]{:T(128)} %bitcast.44, f32[]{:T(128)} %bitcast.45, f32[50,66,2048]{2,1,0:T(8,128)} %get-tuple-element.322, s32[]{:T(128)S(6)} %add.257, ...), kind=kLoop, calls=%fused_computation.8.clone.1 | loop fusion | flops 18743296 | bytes 17301532 | tf_op jit(solution)/shard_map/while/body/eval_jaxpr/stack | solution.py:46
  266.6 13.8 %negate_exponential_fusion.3 = f32[8,64,2048]{2,1,0:T(8,128)S(1)} fusion(f32[64,2048]{1,0:T(8,128)S(1)} %get-tuple-element.285, f32[50,66,2048]{2,1,0:T(8,128)} %get-tuple-element.322, s32[]{:T(128)S(6)} %add.257, s32[]{:T(128)S(6)} %add.258, f32[]{:T(128)} %get-tuple-element.320), kind=kOutput, calls=%fused_computation.12.clone.1 | output fusion | flops 17825792 | bytes 8913416 | tf_op jit(solution)/shard_map/while/body/eval_jaxpr/jit(cumsum)/reduce_window_sum | solution.py:71
  286.1 8.3 %fusion.22 = (f32[8,64,2047]{2,1,0:T(8,128)}, f32[8,64,2047]{2,1,0:T(8,128)}) fusion(f32[50,66,2048]{2,1,0:T(8,128)} %get-tuple-element.322, s32[]{:T(128)S(6)} %add.257, s32[]{:T(128)S(6)} %add.258), kind=kLoop, calls=%fused_computation.31.clone.1 | loop fusion | bytes 16769032 | tf_op jit(solution)/shard_map/while/body/eval_jaxpr/slice | solution.py:26
  295.0 18.2 %multiply_bitcast_fusion.5 = (f32[1,8,64,2048]{3,2,1,0:T(8,128)}, f32[8,64,2048]{2,1,0:T(8,128)S(1)}) fusion(f32[]{:T(128)} %bitcast.41, f32[]{:T(128)} %bitcast.42, f32[50,66,2048]{2,1,0:T(8,128)} %get-tuple-element.322, s32[]{:T(128)S(6)} %add.257, s32[]{:T(128)S(6)} %add.258, f32[]{:T(128)} %get-tuple-element.320, f32[]{:T(128)} %get-tuple-element.325, ...), kind=kLoop, calls=%fused_computation.9.clone.1 | loop fusion | flops 36700160 | bytes 37744680 | tf_op jit(solution)/shard_map/while/body/eval_jaxpr/stack | solution.py:46
  313.3 10.4 %multiply_bitcast_fusion.6 = (f32[1,8,64,2048]{3,2,1,0:T(8,128)}, f32[1,8,64,2048]{3,2,1,0:T(8,128)}, f32[64,2048]{1,0:T(8,128)S(1)}) fusion(f32[8,64,2048]{2,1,0:T(8,128)S(1)} %get-tuple-element.276, f32[]{:T(128)} %bitcast.44, f32[]{:T(128)} %bitcast.45, f32[50,66,2048]{2,1,0:T(8,128)} %get-tuple-element.322, s32[]{:T(128)S(6)} %add.257, ...), kind=kLoop, calls=%fused_computation.8.clone.1 | loop fusion | flops 18743296 | bytes 17301532 | tf_op jit(solution)/shard_map/while/body/eval_jaxpr/stack | solution.py:46
  323.9 14.1 %negate_exponential_fusion.3 = f32[8,64,2048]{2,1,0:T(8,128)S(1)} fusion(f32[64,2048]{1,0:T(8,128)S(1)} %get-tuple-element.285, f32[50,66,2048]{2,1,0:T(8,128)} %get-tuple-element.322, s32[]{:T(128)S(6)} %add.257, s32[]{:T(128)S(6)} %add.258, f32[]{:T(128)} %get-tuple-element.320), kind=kOutput, calls=%fused_computation.12.clone.1 | output fusion | flops 17825792 | bytes 8913416 | tf_op jit(solution)/shard_map/while/body/eval_jaxpr/jit(cumsum)/reduce_window_sum | solution.py:71
  343.7 8.3 %fusion.22 = (f32[8,64,2047]{2,1,0:T(8,128)}, f32[8,64,2047]{2,1,0:T(8,128)}) fusion(f32[50,66,2048]{2,1,0:T(8,128)} %get-tuple-element.322, s32[]{:T(128)S(6)} %add.257, s32[]{:T(128)S(6)} %add.258), kind=kLoop, calls=%fused_computation.31.clone.1 | loop fusion | bytes 16769032 | tf_op jit(solution)/shard_map/while/body/eval_jaxpr/slice | solution.py:26
  352.6 18.4 %multiply_bitcast_fusion.5 = (f32[1,8,64,2048]{3,2,1,0:T(8,128)}, f32[8,64,2048]{2,1,0:T(8,128)S(1)}) fusion(f32[]{:T(128)} %bitcast.41, f32[]{:T(128)} %bitcast.42, f32[50,66,2048]{2,1,0:T(8,128)} %get-tuple-element.322, s32[]{:T(128)S(6)} %add.257, s32[]{:T(128)S(6)} %add.258, f32[]{:T(128)} %get-tuple-element.320, f32[]{:T(128)} %get-tuple-element.325, ...), kind=kLoop, calls=%fused_computation.9.clone.1 | loop fusion | flops 36700160 | bytes 37744680 | tf_op jit(solution)/shard_map/while/body/eval_jaxpr/stack | solution.py:46
  371.0 10.4 %multiply_bitcast_fusion.6 = (f32[1,8,64,2048]{3,2,1,0:T(8,128)}, f32[1,8,64,2048]{3,2,1,0:T(8,128)}, f32[64,2048]{1,0:T(8,128)S(1)}) fusion(f32[8,64,2048]{2,1,0:T(8,128)S(1)} %get-tuple-element.276, f32[]{:T(128)} %bitcast.44, f32[]{:T(128)} %bitcast.45, f32[50,66,2048]{2,1,0:T(8,128)} %get-tuple-element.322, s32[]{:T(128)S(6)} %add.257, ...), kind=kLoop, calls=%fused_computation.8.clone.1 | loop fusion | flops 18743296 | bytes 17301532 | tf_op jit(solution)/shard_map/while/body/eval_jaxpr/stack | solution.py:46
  381.6 13.9 %negate_exponential_fusion.3 = f32[8,64,2048]{2,1,0:T(8,128)S(1)} fusion(f32[64,2048]{1,0:T(8,128)S(1)} %get-tuple-element.285, f32[50,66,2048]{2,1,0:T(8,128)} %get-tuple-element.322, s32[]{:T(128)S(6)} %add.257, s32[]{:T(128)S(6)} %add.258, f32[]{:T(128)} %get-tuple-element.320), kind=kOutput, calls=%fused_computation.12.clone.1 | output fusion | flops 17825792 | bytes 8913416 | tf_op jit(solution)/shard_map/while/body/eval_jaxpr/jit(cumsum)/reduce_window_sum | solution.py:71
  408.8 6.8 %reshape.30 = f32[8,1,65536]{2,1,0:T(1,128)S(1)} reshape(f32[2048,1,4,64]{3,2,1,0:T(4,128)} %fusion.14) | data formatting | bytes 4194304
  415.6 42.5 %all_to_all.18 = f32[8,1,65536]{2,1,0:T(1,128)} all-to-all(f32[8,1,65536]{2,1,0:T(1,128)S(1)} %reshape.30), channel_id=1, replica_groups=mesh['depth'=8,'row'=16] {'depth'}, dimensions={0} | all-to-all | bytes 4194304 | tf_op jit(solution)/shard_map/all_to_all | solution.py:84
  458.6 7.2 %reduce.1 = f32[8,65536]{1,0:T(8,128)S(1)} reduce(f32[8,1,65536]{2,1,0:T(1,128)} %all_to_all.18, f32[]{:T(128)} %broadcast.78), dimensions={1}, to_apply=%all_to_all.13.reduce_sub_computation | reduce | bytes 4194308 | tf_op jit(solution)/shard_map/all_to_all | solution.py:84
  470.6 7.7 %negate_exponential_fusion.1 = (f32[8,1,64,256]{2,1,3,0:T(1,128)S(1)}, f32[64,256]{0,1:T(8,128)S(1)}) fusion(f32[8,4,64,256]{2,1,3,0:T(4,128)} %bitcast.48), kind=kOutput, calls=%fused_computation.21 | output fusion | flops 1294336 | bytes 2686976 | tf_op jit(solution)/shard_map/jit(cumsum)/reduce_window_sum | solution.py:54
  (82 shorter events, 70.6 us)
Async XLA Ops:
  1.3 3.3 collective-permute-start
  3.1 12.2 %collective-permute-start.1 = (f32[1,64,2048]{2,1,0:T(8,128)S(1)}, f32[1,64,2048]{2,1,0:T(8,128)S(1)}, u32[]{:S(2)}, u32[]{:S(2)}) collective-permute-start(f32[1,64,2048]{2,1,0:T(8,128)S(1)} %get-tuple-element.196), channel_id=1, source_target_pairs={{16,0},{32,16},{48,32},{64,48},{80,64},{96,80},{112,96},{17,1},{33... | collective-permute-start | bytes 1572872 | tf_op jit(solution)/shard_map/ppermute | solution.py:17
  4.6 22.1 %copy-start.3 = (f32[8]{0:T(128)S(1)}, f32[8]{0:T(128)}, u32[]{:S(2)}) copy-start(f32[8]{0:T(128)} %param.5) | copy-start | bytes 100
  15.3 8.6 %copy-start.2 = (f32[50,64,2048]{2,1,0:T(8,128)}, f32[50,64,2048]{2,1,0:T(8,128)S(1)}, u32[]{:S(2)}) copy-start(f32[50,64,2048]{2,1,0:T(8,128)S(1)} %constant_dynamic-update-slice_fusion) | copy-start | bytes 78643200
  16.1 12.5 %collective-permute-start.2 = (f32[50,1,2048]{2,1,0:T(1,128)S(1)}, f32[50,1,2048]{2,1,0:T(1,128)S(1)}, u32[]{:S(2)}, u32[]{:S(2)}) collective-permute-start(f32[50,1,2048]{2,1,0:T(1,128)S(1)} %get-tuple-element.194), channel_id=1, source_target_pairs={{0,1},{1,2},{2,3},{3,4},{4,5},{5,6},{6,7},{7,8},{8,9},{9,10},{10,1... | collective-permute-start | bytes 1228808 | tf_op jit(solution)/shard_map/ppermute | solution.py:15
  24.0 12.0 %collective-permute-start.3 = (f32[50,1,2048]{2,1,0:T(1,128)S(1)}, f32[50,1,2048]{2,1,0:T(1,128)}, u32[]{:S(2)}, u32[]{:S(2)}) collective-permute-start(f32[50,1,2048]{2,1,0:T(1,128)S(1)} %get-tuple-element.195), channel_id=1, source_target_pairs={{1,0},{2,1},{3,2},{4,3},{5,4},{6,5},{7,6},{8,7},{9,8},{10,9},{11,1... | collective-permute-start | bytes 1228808 | tf_op jit(solution)/shard_map/ppermute | solution.py:17
  95.5 12.9 %copy-start = (f32[1,8,64,2048]{3,2,1,0:T(8,128)S(1)}, f32[1,8,64,2048]{3,2,1,0:T(8,128)}, u32[]{:S(2)}) copy-start(f32[1,8,64,2048]{3,2,1,0:T(8,128)} %get-tuple-element.283) | copy-start | bytes 12582916 | tf_op jit(solution)/shard_map/while
  95.5 12.9 %copy-start.1 = (f32[1,8,64,2048]{3,2,1,0:T(8,128)S(1)}, f32[1,8,64,2048]{3,2,1,0:T(8,128)}, u32[]{:S(2)}) copy-start(f32[1,8,64,2048]{3,2,1,0:T(8,128)} %get-tuple-element.282) | copy-start | bytes 12582916 | tf_op jit(solution)/shard_map/while
  151.8 14.1 %copy-start = (f32[1,8,64,2048]{3,2,1,0:T(8,128)S(1)}, f32[1,8,64,2048]{3,2,1,0:T(8,128)}, u32[]{:S(2)}) copy-start(f32[1,8,64,2048]{3,2,1,0:T(8,128)} %get-tuple-element.283) | copy-start | bytes 12582916 | tf_op jit(solution)/shard_map/while
  151.8 14.1 %copy-start.1 = (f32[1,8,64,2048]{3,2,1,0:T(8,128)S(1)}, f32[1,8,64,2048]{3,2,1,0:T(8,128)}, u32[]{:S(2)}) copy-start(f32[1,8,64,2048]{3,2,1,0:T(8,128)} %get-tuple-element.282) | copy-start | bytes 12582916 | tf_op jit(solution)/shard_map/while
  209.3 14.2 %copy-start = (f32[1,8,64,2048]{3,2,1,0:T(8,128)S(1)}, f32[1,8,64,2048]{3,2,1,0:T(8,128)}, u32[]{:S(2)}) copy-start(f32[1,8,64,2048]{3,2,1,0:T(8,128)} %get-tuple-element.283) | copy-start | bytes 12582916 | tf_op jit(solution)/shard_map/while
  209.3 14.2 %copy-start.1 = (f32[1,8,64,2048]{3,2,1,0:T(8,128)S(1)}, f32[1,8,64,2048]{3,2,1,0:T(8,128)}, u32[]{:S(2)}) copy-start(f32[1,8,64,2048]{3,2,1,0:T(8,128)} %get-tuple-element.282) | copy-start | bytes 12582916 | tf_op jit(solution)/shard_map/while
  266.6 13.8 %copy-start = (f32[1,8,64,2048]{3,2,1,0:T(8,128)S(1)}, f32[1,8,64,2048]{3,2,1,0:T(8,128)}, u32[]{:S(2)}) copy-start(f32[1,8,64,2048]{3,2,1,0:T(8,128)} %get-tuple-element.283) | copy-start | bytes 12582916 | tf_op jit(solution)/shard_map/while
  266.6 13.8 %copy-start.1 = (f32[1,8,64,2048]{3,2,1,0:T(8,128)S(1)}, f32[1,8,64,2048]{3,2,1,0:T(8,128)}, u32[]{:S(2)}) copy-start(f32[1,8,64,2048]{3,2,1,0:T(8,128)} %get-tuple-element.282) | copy-start | bytes 12582916 | tf_op jit(solution)/shard_map/while
  323.9 14.2 %copy-start = (f32[1,8,64,2048]{3,2,1,0:T(8,128)S(1)}, f32[1,8,64,2048]{3,2,1,0:T(8,128)}, u32[]{:S(2)}) copy-start(f32[1,8,64,2048]{3,2,1,0:T(8,128)} %get-tuple-element.283) | copy-start | bytes 12582916 | tf_op jit(solution)/shard_map/while
  323.9 14.2 %copy-start.1 = (f32[1,8,64,2048]{3,2,1,0:T(8,128)S(1)}, f32[1,8,64,2048]{3,2,1,0:T(8,128)}, u32[]{:S(2)}) copy-start(f32[1,8,64,2048]{3,2,1,0:T(8,128)} %get-tuple-element.282) | copy-start | bytes 12582916 | tf_op jit(solution)/shard_map/while
  381.6 13.9 %copy-start = (f32[1,8,64,2048]{3,2,1,0:T(8,128)S(1)}, f32[1,8,64,2048]{3,2,1,0:T(8,128)}, u32[]{:S(2)}) copy-start(f32[1,8,64,2048]{3,2,1,0:T(8,128)} %get-tuple-element.283) | copy-start | bytes 12582916 | tf_op jit(solution)/shard_map/while
  381.6 13.9 %copy-start.1 = (f32[1,8,64,2048]{3,2,1,0:T(8,128)S(1)}, f32[1,8,64,2048]{3,2,1,0:T(8,128)}, u32[]{:S(2)}) copy-start(f32[1,8,64,2048]{3,2,1,0:T(8,128)} %get-tuple-element.282) | copy-start | bytes 12582916 | tf_op jit(solution)/shard_map/while
where the time goes:
time: 484 us; the launch traced here: 483 us
  other arithmetic  327 us (68%)
  local copies, waits for them, and re-layouts  91.4 us (19%)
  blocking collectives  42.5 us (9%)
  starting transfers between devices  9.19 us (2%)
  waiting for transfers between devices  7.54 us (2%)
    another operation x12, other arithmetic, emit(): jnp.stack([(transfer[channel] + transfer[3 + channel] * tinting) * weight...  172 us
    another operation x6, other arithmetic, march(): before = jnp.cumsum(depth_term, 0) - depth_term  83 us
    slice x6, local copies, waits for them, and re-layouts, slope_cols(): right = jnp.concatenate([center[..., 1:], zero_col], -1)  49.7 us
    all_to_all x1, blocking collectives, on_device(): lax.all_to_all(partial_image[None], 'depth', split_axis=3, concat_axis=0,...  42.5 us
    unnamed x8, local copies, waits for them, and re-layouts  26.7 us
    reduce_sum x6, other arithmetic, march(): color = color + jnp.sum(passing[None] * emitted, 1)  23.7 us
    concatenate x1, other arithmetic, with_halo(): jnp.concatenate([lax.ppermute(tail, axis, [(i, (i + 1) % count) for i in...  20.7 us
  transfers between devices with their start and end apart: 4, of which 2 were waited for; matrix products, arithmetic and copies ran while one was open for 2% of the time, Pallas kernels for 0%

commit v1 on v0

--- a/solution.py
+++ b/solution.py
@@ -1,7 +1,41 @@
+import functools
 import jax
 import jax.numpy as jnp
 from jax import lax
 from jax.sharding import PartitionSpec as P
+
+
+def form_weights(u, on_dim, original):
+    side_arr = u.shape
+    block_out = u.reshape(
+        *side_arr[:on_dim], original, side_arr[on_dim] // original, *side_arr[on_dim + 1 :]
+    )
+    y2 = jnp.moveaxis(block_out, on_dim, 0)
+    return y2
+
+
+def draw_run_up(mine_x, axis_no):
+    e_next = list(mine_x.shape[1:])
+    e_next[axis_no] *= mine_x.shape[0]
+    piece_now = jnp.moveaxis(mine_x, 0, axis_no).reshape(e_next)
+    return piece_now
+
+
+def perform_the_pages(local_block, dev_axis, m, target):
+    near, last = (lax.axis_size(dev_axis), lax.axis_index(dev_axis))
+    g_now = form_weights(local_block, m, near)
+    d = 1
+    nodes = [g_now[last]]
+    while d < near:
+        z = g_now[last ^ d]
+        nodes.append(lax.ppermute(z, dev_axis, [(no, no ^ d) for no in range(near)]))
+        d = d + 1
+    g_now = jnp.stack(nodes, axis=0)[last ^ jnp.arange(near)]
+    part_now = draw_run_up(g_now, target)
+    return part_now
+
+
+get_the_space = functools.partial(perform_the_pages, dev_axis="depth", m=3, target=0)
 
 
 def with_halo(cells, sides, width):
@@ -80,9 +114,7 @@
         march, (start_color, start_depth), jnp.arange(steps, dtype=jnp.int32)
     )
     partial_image = jnp.concatenate([color, depth_acc[None]], 0)
-    final = blend_parts(
-        lax.all_to_all(partial_image[None], "depth", split_axis=3, concat_axis=0, tiled=True)
-    )
+    final = blend_parts(get_the_space(partial_image[None]))
     return jnp.concatenate([final[:3], -jnp.expm1(-final[3:4])], 0)
 
 

time: 484 us -> 460 us (0.950)
  blocking collectives: 42.5 us -> 0 us
  waiting for transfers between devices: 7.54 us -> 30 us
  other arithmetic: 327 us -> 307 us
  starting transfers between devices: 9.19 us -> 27.9 us
  local copies, waits for them, and re-layouts: 91.4 us -> 86.1 us
    all_to_all x1 -> x0, blocking collectives: 42.5 us -> none  [on_device(): lax.all_to_all(partial_image[None], 'depth', split_axis=3, concat_axis=0,...]
    ppermute x0 -> x7, waiting for transfers between devices: none -> 22.3 us  [perform_the_pages(): lax.ppermute(z, dev_axis, [(no, no ^ d) for no in range(near)])]
    ppermute x0 -> x7, starting transfers between devices: none -> 19 us  [perform_the_pages(): lax.ppermute(z, dev_axis, [(no, no ^ d) for no in range(near)])]
    another operation x1, other arithmetic: 7.68 us -> 0.14 us  [blend_parts(): before = jnp.cumsum(depth_parts, 0) - depth_parts]
    all_to_all x1 -> x0, other arithmetic: 7.22 us -> none  [on_device(): lax.all_to_all(partial_image[None], 'depth', split_axis=3, concat_axis=0,...]
    unnamed x3 -> x2, other arithmetic: 5.27 us -> 0.01 us
    unnamed x8 -> x18, local copies, waits for them, and re-layouts: 26.7 us -> 22.1 us
  transfers between devices with their start and end apart: 4 -> 11, of which waited for: 2 -> 8; matrix products, arithmetic and copies ran while one was open for 2% -> 3% of each run, Pallas kernels for 0% -> 0%
where the time goes in v1:
time: 460 us; the launch traced here: 458 us
  other arithmetic  307 us (67%)
  local copies, waits for them, and re-layouts  86.1 us (19%)
  waiting for transfers between devices  30 us (7%)
  starting transfers between devices  27.9 us (6%)
  loops' own time  4.87 us (1%)
    another operation x12, other arithmetic, emit(): jnp.stack([(transfer[channel] + transfer[3 + channel] * tinting) * weight...  173 us
    another operation x6, other arithmetic, march(): before = jnp.cumsum(depth_term, 0) - depth_term  84.5 us
    slice x6, local copies, waits for them, and re-layouts, slope_cols(): right = jnp.concatenate([center[..., 1:], zero_col], -1)  49.8 us
    reduce_sum x6, other arithmetic, march(): color = color + jnp.sum(passing[None] * emitted, 1)  23.7 us
    ppermute x7, waiting for transfers between devices, perform_the_pages(): lax.ppermute(z, dev_axis, [(no, no ^ d) for no in range(near)])  22.3 us
    unnamed x18, local copies, waits for them, and re-layouts  22.1 us
    concatenate x1, other arithmetic, with_halo(): jnp.concatenate([lax.ppermute(tail, axis, [(i, (i + 1) % count) for i in...  20.7 us
    ppermute x7, starting transfers between devices, perform_the_pages(): lax.ppermute(z, dev_axis, [(no, no ^ d) for no in range(near)])  19 us
  transfers between devices with their start and end apart: 11, of which 8 were waited for; matrix products, arithmetic and copies ran while one was open for 3% of the time, Pallas kernels for 0%

profile of v1, /device:TPU:14, one launch (start us, length us, event | category | flops | bytes accessed | tf_op | source)
XLA Modules:
  0.0 457.9 jit_solution(15560646196273231076)
XLA Ops:
  4.6 10.6 %constant_dynamic-update-slice_fusion.1 = f32[50,64,2048]{2,1,0:T(8,128)S(1)} fusion(f32[50,64,2048]{2,1,0:T(8,128)S(1)} %constant_dynamic-update-slice_fusion.2, f32[48,64,2048]{2,1,0:T(8,128)} %param.4), kind=kLoop, calls=%fused_computation.47 | loop fusion | bytes 50331648
  15.3 8.6 %copy-done.2 = f32[50,64,2048]{2,1,0:T(8,128)} copy-done((f32[50,64,2048]{2,1,0:T(8,128)}, f32[50,64,2048]{2,1,0:T(8,128)S(1)}, u32[]{:S(2)}) %copy-start.2) | copy-done | bytes 26214424
  34.6 5.6 %collective-permute-done.3 = f32[50,1,2048]{2,1,0:T(1,128)} collective-permute-done((f32[50,1,2048]{2,1,0:T(1,128)S(1)}, f32[50,1,2048]{2,1,0:T(1,128)}, u32[]{:S(2)}, u32[]{:S(2)}) %collective-permute-start.3) | collective-permute-done | bytes 409632 | tf_op jit(solution)/shard_map/ppermute | solution.py:51
  40.2 20.7 %pad_maximum_fusion = f32[50,66,2048]{2,1,0:T(8,128)} fusion(f32[50,1,2048]{2,1,0:T(1,128)} %collective-permute-done.3, f32[50,64,2048]{2,1,0:T(8,128)} %copy-done.2, f32[50,1,2048]{2,1,0:T(1,128)S(1)} %collective-permute-done.2), kind=kLoop, calls=%fused_computation.18 | loop fusion | flops 13516800 | bytes 54067200 | tf_op jit(solution)/shard_map/concatenate | solution.py:47
  60.9 348.4 %while.16 = (s32[]{:T(128)}, f32[3,64,2048]{2,1,0:T(8,128)S(1)}, f32[64,2048]{1,0:T(8,128)S(1)}, f32[]{:T(128)}, s32[6]{0:T(128)S(1)}, /*index=5*/f32[50,66,2048...) while((s32[]{:T(128)}, f32[3,64,2048]{2,1,0:T(8,128)S(1)}, ...), condition=%wide.region_4.5_spmd.clone, body=%wide.region_0.4_spmd.clone.sunk | while | flops 86507528 | bytes 139449296 | solution.py:113
  62.2 8.3 %fusion.24 = (f32[8,64,2047]{2,1,0:T(8,128)}, f32[8,64,2047]{2,1,0:T(8,128)}) fusion(f32[50,66,2048]{2,1,0:T(8,128)} %get-tuple-element.327, s32[]{:T(128)S(6)} %add.302, s32[]{:T(128)S(6)} %add.303), kind=kLoop, calls=%fused_computation.53.clone.1 | loop fusion | bytes 16769032 | tf_op jit(solution)/shard_map/while/body/eval_jaxpr/slice | solution.py:60
  71.2 18.1 %multiply_bitcast_fusion.5 = (f32[1,8,64,2048]{3,2,1,0:T(8,128)}, f32[8,64,2048]{2,1,0:T(8,128)S(1)}) fusion(f32[]{:T(128)} %bitcast.70, f32[]{:T(128)} %bitcast.71, f32[50,66,2048]{2,1,0:T(8,128)} %get-tuple-element.327, s32[]{:T(128)S(6)} %add.302, s32[]{:T(128)S(6)} %add.303, f32[]{:T(128)} %get-tuple-element.325, f32[]{:T(128)} %get-tuple-element.330, ...), kind=kLoop, calls=%fused_computation.10.clone.1 | loop fusion | flops 36700160 | bytes 37744680 | tf_op jit(solution)/shard_map/while/body/eval_jaxpr/stack | solution.py:80
  89.3 10.6 %multiply_bitcast_fusion.6 = (f32[1,8,64,2048]{3,2,1,0:T(8,128)}, f32[1,8,64,2048]{3,2,1,0:T(8,128)}, f32[64,2048]{1,0:T(8,128)S(1)}) fusion(f32[8,64,2048]{2,1,0:T(8,128)S(1)} %get-tuple-element.281, f32[]{:T(128)} %bitcast.73, f32[]{:T(128)} %bitcast.74, f32[50,66,2048]{2,1,0:T(8,128)} %get-tuple-element.327, s32[]{:T(128)S(6)} %add.302, ...), kind=kLoop, calls=%fused_computation.9.clone.1 | loop fusion | flops 18743296 | bytes 17301532 | tf_op jit(solution)/shard_map/while/body/eval_jaxpr/stack | solution.py:80
  100.1 13.2 %negate_exponential_fusion.2 = f32[8,64,2048]{2,1,0:T(8,128)S(1)} fusion(f32[64,2048]{1,0:T(8,128)S(1)} %get-tuple-element.290, f32[50,66,2048]{2,1,0:T(8,128)} %get-tuple-element.327, s32[]{:T(128)S(6)} %add.302, s32[]{:T(128)S(6)} %add.303, f32[]{:T(128)} %get-tuple-element.325), kind=kOutput, calls=%fused_computation.13.clone.1 | output fusion | flops 17825792 | bytes 8913416 | tf_op jit(solution)/shard_map/while/body/eval_jaxpr/jit(cumsum)/reduce_window_sum | solution.py:105
  119.3 8.3 %fusion.24 = (f32[8,64,2047]{2,1,0:T(8,128)}, f32[8,64,2047]{2,1,0:T(8,128)}) fusion(f32[50,66,2048]{2,1,0:T(8,128)} %get-tuple-element.327, s32[]{:T(128)S(6)} %add.302, s32[]{:T(128)S(6)} %add.303), kind=kLoop, calls=%fused_computation.53.clone.1 | loop fusion | bytes 16769032 | tf_op jit(solution)/shard_map/while/body/eval_jaxpr/slice | solution.py:60
  128.3 18.4 %multiply_bitcast_fusion.5 = (f32[1,8,64,2048]{3,2,1,0:T(8,128)}, f32[8,64,2048]{2,1,0:T(8,128)S(1)}) fusion(f32[]{:T(128)} %bitcast.70, f32[]{:T(128)} %bitcast.71, f32[50,66,2048]{2,1,0:T(8,128)} %get-tuple-element.327, s32[]{:T(128)S(6)} %add.302, s32[]{:T(128)S(6)} %add.303, f32[]{:T(128)} %get-tuple-element.325, f32[]{:T(128)} %get-tuple-element.330, ...), kind=kLoop, calls=%fused_computation.10.clone.1 | loop fusion | flops 36700160 | bytes 37744680 | tf_op jit(solution)/shard_map/while/body/eval_jaxpr/stack | solution.py:80
  146.6 10.6 %multiply_bitcast_fusion.6 = (f32[1,8,64,2048]{3,2,1,0:T(8,128)}, f32[1,8,64,2048]{3,2,1,0:T(8,128)}, f32[64,2048]{1,0:T(8,128)S(1)}) fusion(f32[8,64,2048]{2,1,0:T(8,128)S(1)} %get-tuple-element.281, f32[]{:T(128)} %bitcast.73, f32[]{:T(128)} %bitcast.74, f32[50,66,2048]{2,1,0:T(8,128)} %get-tuple-element.327, s32[]{:T(128)S(6)} %add.302, ...), kind=kLoop, calls=%fused_computation.9.clone.1 | loop fusion | flops 18743296 | bytes 17301532 | tf_op jit(solution)/shard_map/while/body/eval_jaxpr/stack | solution.py:80
  157.4 14.3 %negate_exponential_fusion.2 = f32[8,64,2048]{2,1,0:T(8,128)S(1)} fusion(f32[64,2048]{1,0:T(8,128)S(1)} %get-tuple-element.290, f32[50,66,2048]{2,1,0:T(8,128)} %get-tuple-element.327, s32[]{:T(128)S(6)} %add.302, s32[]{:T(128)S(6)} %add.303, f32[]{:T(128)} %get-tuple-element.325), kind=kOutput, calls=%fused_computation.13.clone.1 | output fusion | flops 17825792 | bytes 8913416 | tf_op jit(solution)/shard_map/while/body/eval_jaxpr/jit(cumsum)/reduce_window_sum | solution.py:105
  177.7 8.3 %fusion.24 = (f32[8,64,2047]{2,1,0:T(8,128)}, f32[8,64,2047]{2,1,0:T(8,128)}) fusion(f32[50,66,2048]{2,1,0:T(8,128)} %get-tuple-element.327, s32[]{:T(128)S(6)} %add.302, s32[]{:T(128)S(6)} %add.303), kind=kLoop, calls=%fused_computation.53.clone.1 | loop fusion | bytes 16769032 | tf_op jit(solution)/shard_map/while/body/eval_jaxpr/slice | solution.py:60
  186.7 18.2 %multiply_bitcast_fusion.5 = (f32[1,8,64,2048]{3,2,1,0:T(8,128)}, f32[8,64,2048]{2,1,0:T(8,128)S(1)}) fusion(f32[]{:T(128)} %bitcast.70, f32[]{:T(128)} %bitcast.71, f32[50,66,2048]{2,1,0:T(8,128)} %get-tuple-element.327, s32[]{:T(128)S(6)} %add.302, s32[]{:T(128)S(6)} %add.303, f32[]{:T(128)} %get-tuple-element.325, f32[]{:T(128)} %get-tuple-element.330, ...), kind=kLoop, calls=%fused_computation.10.clone.1 | loop fusion | flops 36700160 | bytes 37744680 | tf_op jit(solution)/shard_map/while/body/eval_jaxpr/stack | solution.py:80
  204.9 10.6 %multiply_bitcast_fusion.6 = (f32[1,8,64,2048]{3,2,1,0:T(8,128)}, f32[1,8,64,2048]{3,2,1,0:T(8,128)}, f32[64,2048]{1,0:T(8,128)S(1)}) fusion(f32[8,64,2048]{2,1,0:T(8,128)S(1)} %get-tuple-element.281, f32[]{:T(128)} %bitcast.73, f32[]{:T(128)} %bitcast.74, f32[50,66,2048]{2,1,0:T(8,128)} %get-tuple-element.327, s32[]{:T(128)S(6)} %add.302, ...), kind=kLoop, calls=%fused_computation.9.clone.1 | loop fusion | flops 18743296 | bytes 17301532 | tf_op jit(solution)/shard_map/while/body/eval_jaxpr/stack | solution.py:80
  215.7 14.2 %negate_exponential_fusion.2 = f32[8,64,2048]{2,1,0:T(8,128)S(1)} fusion(f32[64,2048]{1,0:T(8,128)S(1)} %get-tuple-element.290, f32[50,66,2048]{2,1,0:T(8,128)} %get-tuple-element.327, s32[]{:T(128)S(6)} %add.302, s32[]{:T(128)S(6)} %add.303, f32[]{:T(128)} %get-tuple-element.325), kind=kOutput, calls=%fused_computation.13.clone.1 | output fusion | flops 17825792 | bytes 8913416 | tf_op jit(solution)/shard_map/while/body/eval_jaxpr/jit(cumsum)/reduce_window_sum | solution.py:105
  235.8 8.3 %fusion.24 = (f32[8,64,2047]{2,1,0:T(8,128)}, f32[8,64,2047]{2,1,0:T(8,128)}) fusion(f32[50,66,2048]{2,1,0:T(8,128)} %get-tuple-element.327, s32[]{:T(128)S(6)} %add.302, s32[]{:T(128)S(6)} %add.303), kind=kLoop, calls=%fused_computation.53.clone.1 | loop fusion | bytes 16769032 | tf_op jit(solution)/shard_map/while/body/eval_jaxpr/slice | solution.py:60
  244.8 18.1 %multiply_bitcast_fusion.5 = (f32[1,8,64,2048]{3,2,1,0:T(8,128)}, f32[8,64,2048]{2,1,0:T(8,128)S(1)}) fusion(f32[]{:T(128)} %bitcast.70, f32[]{:T(128)} %bitcast.71, f32[50,66,2048]{2,1,0:T(8,128)} %get-tuple-element.327, s32[]{:T(128)S(6)} %add.302, s32[]{:T(128)S(6)} %add.303, f32[]{:T(128)} %get-tuple-element.325, f32[]{:T(128)} %get-tuple-element.330, ...), kind=kLoop, calls=%fused_computation.10.clone.1 | loop fusion | flops 36700160 | bytes 37744680 | tf_op jit(solution)/shard_map/while/body/eval_jaxpr/stack | solution.py:80
  262.8 10.6 %multiply_bitcast_fusion.6 = (f32[1,8,64,2048]{3,2,1,0:T(8,128)}, f32[1,8,64,2048]{3,2,1,0:T(8,128)}, f32[64,2048]{1,0:T(8,128)S(1)}) fusion(f32[8,64,2048]{2,1,0:T(8,128)S(1)} %get-tuple-element.281, f32[]{:T(128)} %bitcast.73, f32[]{:T(128)} %bitcast.74, f32[50,66,2048]{2,1,0:T(8,128)} %get-tuple-element.327, s32[]{:T(128)S(6)} %add.302, ...), kind=kLoop, calls=%fused_computation.9.clone.1 | loop fusion | flops 18743296 | bytes 17301532 | tf_op jit(solution)/shard_map/while/body/eval_jaxpr/stack | solution.py:80
  273.6 14.2 %negate_exponential_fusion.2 = f32[8,64,2048]{2,1,0:T(8,128)S(1)} fusion(f32[64,2048]{1,0:T(8,128)S(1)} %get-tuple-element.290, f32[50,66,2048]{2,1,0:T(8,128)} %get-tuple-element.327, s32[]{:T(128)S(6)} %add.302, s32[]{:T(128)S(6)} %add.303, f32[]{:T(128)} %get-tuple-element.325), kind=kOutput, calls=%fused_computation.13.clone.1 | output fusion | flops 17825792 | bytes 8913416 | tf_op jit(solution)/shard_map/while/body/eval_jaxpr/jit(cumsum)/reduce_window_sum | solution.py:105
  293.8 8.3 %fusion.24 = (f32[8,64,2047]{2,1,0:T(8,128)}, f32[8,64,2047]{2,1,0:T(8,128)}) fusion(f32[50,66,2048]{2,1,0:T(8,128)} %get-tuple-element.327, s32[]{:T(128)S(6)} %add.302, s32[]{:T(128)S(6)} %add.303), kind=kLoop, calls=%fused_computation.53.clone.1 | loop fusion | bytes 16769032 | tf_op jit(solution)/shard_map/while/body/eval_jaxpr/slice | solution.py:60
  302.8 18.6 %multiply_bitcast_fusion.5 = (f32[1,8,64,2048]{3,2,1,0:T(8,128)}, f32[8,64,2048]{2,1,0:T(8,128)S(1)}) fusion(f32[]{:T(128)} %bitcast.70, f32[]{:T(128)} %bitcast.71, f32[50,66,2048]{2,1,0:T(8,128)} %get-tuple-element.327, s32[]{:T(128)S(6)} %add.302, s32[]{:T(128)S(6)} %add.303, f32[]{:T(128)} %get-tuple-element.325, f32[]{:T(128)} %get-tuple-element.330, ...), kind=kLoop, calls=%fused_computation.10.clone.1 | loop fusion | flops 36700160 | bytes 37744680 | tf_op jit(solution)/shard_map/while/body/eval_jaxpr/stack | solution.py:80
  321.3 10.6 %multiply_bitcast_fusion.6 = (f32[1,8,64,2048]{3,2,1,0:T(8,128)}, f32[1,8,64,2048]{3,2,1,0:T(8,128)}, f32[64,2048]{1,0:T(8,128)S(1)}) fusion(f32[8,64,2048]{2,1,0:T(8,128)S(1)} %get-tuple-element.281, f32[]{:T(128)} %bitcast.73, f32[]{:T(128)} %bitcast.74, f32[50,66,2048]{2,1,0:T(8,128)} %get-tuple-element.327, s32[]{:T(128)S(6)} %add.302, ...), kind=kLoop, calls=%fused_computation.9.clone.1 | loop fusion | flops 18743296 | bytes 17301532 | tf_op jit(solution)/shard_map/while/body/eval_jaxpr/stack | solution.py:80
  332.1 14.2 %negate_exponential_fusion.2 = f32[8,64,2048]{2,1,0:T(8,128)S(1)} fusion(f32[64,2048]{1,0:T(8,128)S(1)} %get-tuple-element.290, f32[50,66,2048]{2,1,0:T(8,128)} %get-tuple-element.327, s32[]{:T(128)S(6)} %add.302, s32[]{:T(128)S(6)} %add.303, f32[]{:T(128)} %get-tuple-element.325), kind=kOutput, calls=%fused_computation.13.clone.1 | output fusion | flops 17825792 | bytes 8913416 | tf_op jit(solution)/shard_map/while/body/eval_jaxpr/jit(cumsum)/reduce_window_sum | solution.py:105
  352.2 8.3 %fusion.24 = (f32[8,64,2047]{2,1,0:T(8,128)}, f32[8,64,2047]{2,1,0:T(8,128)}) fusion(f32[50,66,2048]{2,1,0:T(8,128)} %get-tuple-element.327, s32[]{:T(128)S(6)} %add.302, s32[]{:T(128)S(6)} %add.303), kind=kLoop, calls=%fused_computation.53.clone.1 | loop fusion | bytes 16769032 | tf_op jit(solution)/shard_map/while/body/eval_jaxpr/slice | solution.py:60
  361.2 18.3 %multiply_bitcast_fusion.5 = (f32[1,8,64,2048]{3,2,1,0:T(8,128)}, f32[8,64,2048]{2,1,0:T(8,128)S(1)}) fusion(f32[]{:T(128)} %bitcast.70, f32[]{:T(128)} %bitcast.71, f32[50,66,2048]{2,1,0:T(8,128)} %get-tuple-element.327, s32[]{:T(128)S(6)} %add.302, s32[]{:T(128)S(6)} %add.303, f32[]{:T(128)} %get-tuple-element.325, f32[]{:T(128)} %get-tuple-element.330, ...), kind=kLoop, calls=%fused_computation.10.clone.1 | loop fusion | flops 36700160 | bytes 37744680 | tf_op jit(solution)/shard_map/while/body/eval_jaxpr/stack | solution.py:80
  379.5 10.6 %multiply_bitcast_fusion.6 = (f32[1,8,64,2048]{3,2,1,0:T(8,128)}, f32[1,8,64,2048]{3,2,1,0:T(8,128)}, f32[64,2048]{1,0:T(8,128)S(1)}) fusion(f32[8,64,2048]{2,1,0:T(8,128)S(1)} %get-tuple-element.281, f32[]{:T(128)} %bitcast.73, f32[]{:T(128)} %bitcast.74, f32[50,66,2048]{2,1,0:T(8,128)} %get-tuple-element.327, s32[]{:T(128)S(6)} %add.302, ...), kind=kLoop, calls=%fused_computation.9.clone.1 | loop fusion | flops 18743296 | bytes 17301532 | tf_op jit(solution)/shard_map/while/body/eval_jaxpr/stack | solution.py:80
  390.3 14.2 %negate_exponential_fusion.2 = f32[8,64,2048]{2,1,0:T(8,128)S(1)} fusion(f32[64,2048]{1,0:T(8,128)S(1)} %get-tuple-element.290, f32[50,66,2048]{2,1,0:T(8,128)} %get-tuple-element.327, s32[]{:T(128)S(6)} %add.302, s32[]{:T(128)S(6)} %add.303, f32[]{:T(128)} %get-tuple-element.325), kind=kOutput, calls=%fused_computation.13.clone.1 | output fusion | flops 17825792 | bytes 8913416 | tf_op jit(solution)/shard_map/while/body/eval_jaxpr/jit(cumsum)/reduce_window_sum | solution.py:105
  411.7 5.4 %collective-permute-start.4 = (f32[1,4,64,256]{3,2,1,0:T(8,128)}, f32[1,4,64,256]{3,2,1,0:T(8,128)S(1)}, u32[]{:S(2)}, u32[]{:S(2)}) collective-permute-start(f32[1,4,64,256]{3,2,1,0:T(8,128)} %get-tuple-element.204), channel_id=1, source_target_pairs={{0,16},{16,0},{32,48},{48,32},{64,80},{80,64},{96,112},{112,96},{1... | collective-permute-start | bytes 786440 | tf_op jit(solution)/shard_map/ppermute | solution.py:31
  417.1 6.6 %collective-permute-start.5 = (f32[1,4,64,256]{3,2,1,0:T(8,128)}, f32[1,4,64,256]{3,2,1,0:T(8,128)S(1)}, u32[]{:S(2)}, u32[]{:S(2)}) collective-permute-start(f32[1,4,64,256]{3,2,1,0:T(8,128)} %get-tuple-element.203), channel_id=1, source_target_pairs={{0,32},{16,48},{32,0},{48,16},{64,96},{80,112},{96,64},{112,80},{1... | collective-permute-start | bytes 786440 | tf_op jit(solution)/shard_map/ppermute | solution.py:31
  436.3 7.7 %collective-permute-done.7 = f32[1,4,64,256]{3,2,1,0:T(8,128)S(1)} collective-permute-done((f32[1,4,64,256]{3,2,1,0:T(8,128)S(1)}, f32[1,4,64,256]{3,2,1,0:T(8,128)S(1)}, u32[]{:S(2)}, u32[]{:S(2)}) %collective-permute-start.7) | collective-permute-done | bytes 262176 | tf_op jit(solution)/shard_map/ppermute | solution.py:31
  (106 shorter events, 78.7 us)
Async XLA Ops:
  1.3 3.3 collective-permute-start
  3.1 12.2 %collective-permute-start.1 = (f32[1,64,2048]{2,1,0:T(8,128)S(1)}, f32[1,64,2048]{2,1,0:T(8,128)S(1)}, u32[]{:S(2)}, u32[]{:S(2)}) collective-permute-start(f32[1,64,2048]{2,1,0:T(8,128)S(1)} %get-tuple-element.196), channel_id=1, source_target_pairs={{16,0},{32,16},{48,32},{64,48},{80,64},{96,80},{112,96},{17,1},{33... | collective-permute-start | bytes 1572872 | tf_op jit(solution)/shard_map/ppermute | solution.py:51
  4.6 26.1 %copy-start.4 = (f32[8]{0:T(128)S(1)}, f32[8]{0:T(128)}, u32[]{:S(2)}) copy-start(f32[8]{0:T(128)} %param.5) | copy-start | bytes 100
  15.3 8.6 %copy-start.2 = (f32[50,64,2048]{2,1,0:T(8,128)}, f32[50,64,2048]{2,1,0:T(8,128)S(1)}, u32[]{:S(2)}) copy-start(f32[50,64,2048]{2,1,0:T(8,128)S(1)} %constant_dynamic-update-slice_fusion) | copy-start | bytes 78643200
  24.7 9.8 %collective-permute-start.2 = (f32[50,1,2048]{2,1,0:T(1,128)S(1)}, f32[50,1,2048]{2,1,0:T(1,128)S(1)}, u32[]{:S(2)}, u32[]{:S(2)}) collective-permute-start(f32[50,1,2048]{2,1,0:T(1,128)S(1)} %get-tuple-element.194), channel_id=1, source_target_pairs={{0,1},{1,2},{2,3},{3,4},{4,5},{5,6},{6,7},{7,8},{8,9},{9,10},{10,1... | collective-permute-start | bytes 1228808 | tf_op jit(solution)/shard_map/ppermute | solution.py:49
  28.1 12.1 %collective-permute-start.3 = (f32[50,1,2048]{2,1,0:T(1,128)S(1)}, f32[50,1,2048]{2,1,0:T(1,128)}, u32[]{:S(2)}, u32[]{:S(2)}) collective-permute-start(f32[50,1,2048]{2,1,0:T(1,128)S(1)} %get-tuple-element.195), channel_id=1, source_target_pairs={{1,0},{2,1},{3,2},{4,3},{5,4},{6,5},{7,6},{8,7},{9,8},{10,9},{11,1... | collective-permute-start | bytes 1228808 | tf_op jit(solution)/shard_map/ppermute | solution.py:51
  100.1 13.3 %copy-start = (f32[1,8,64,2048]{3,2,1,0:T(8,128)S(1)}, f32[1,8,64,2048]{3,2,1,0:T(8,128)}, u32[]{:S(2)}) copy-start(f32[1,8,64,2048]{3,2,1,0:T(8,128)} %get-tuple-element.288) | copy-start | bytes 12582916 | tf_op jit(solution)/shard_map/while
  100.1 13.3 %copy-start.1 = (f32[1,8,64,2048]{3,2,1,0:T(8,128)S(1)}, f32[1,8,64,2048]{3,2,1,0:T(8,128)}, u32[]{:S(2)}) copy-start(f32[1,8,64,2048]{3,2,1,0:T(8,128)} %get-tuple-element.287) | copy-start | bytes 12582916 | tf_op jit(solution)/shard_map/while
  157.4 14.4 %copy-start = (f32[1,8,64,2048]{3,2,1,0:T(8,128)S(1)}, f32[1,8,64,2048]{3,2,1,0:T(8,128)}, u32[]{:S(2)}) copy-start(f32[1,8,64,2048]{3,2,1,0:T(8,128)} %get-tuple-element.288) | copy-start | bytes 12582916 | tf_op jit(solution)/shard_map/while
  157.4 14.4 %copy-start.1 = (f32[1,8,64,2048]{3,2,1,0:T(8,128)S(1)}, f32[1,8,64,2048]{3,2,1,0:T(8,128)}, u32[]{:S(2)}) copy-start(f32[1,8,64,2048]{3,2,1,0:T(8,128)} %get-tuple-element.287) | copy-start | bytes 12582916 | tf_op jit(solution)/shard_map/while
  215.6 14.2 %copy-start = (f32[1,8,64,2048]{3,2,1,0:T(8,128)S(1)}, f32[1,8,64,2048]{3,2,1,0:T(8,128)}, u32[]{:S(2)}) copy-start(f32[1,8,64,2048]{3,2,1,0:T(8,128)} %get-tuple-element.288) | copy-start | bytes 12582916 | tf_op jit(solution)/shard_map/while
  215.7 14.2 %copy-start.1 = (f32[1,8,64,2048]{3,2,1,0:T(8,128)S(1)}, f32[1,8,64,2048]{3,2,1,0:T(8,128)}, u32[]{:S(2)}) copy-start(f32[1,8,64,2048]{3,2,1,0:T(8,128)} %get-tuple-element.287) | copy-start | bytes 12582916 | tf_op jit(solution)/shard_map/while
  273.6 14.3 %copy-start = (f32[1,8,64,2048]{3,2,1,0:T(8,128)S(1)}, f32[1,8,64,2048]{3,2,1,0:T(8,128)}, u32[]{:S(2)}) copy-start(f32[1,8,64,2048]{3,2,1,0:T(8,128)} %get-tuple-element.288) | copy-start | bytes 12582916 | tf_op jit(solution)/shard_map/while
  273.6 14.3 %copy-start.1 = (f32[1,8,64,2048]{3,2,1,0:T(8,128)S(1)}, f32[1,8,64,2048]{3,2,1,0:T(8,128)}, u32[]{:S(2)}) copy-start(f32[1,8,64,2048]{3,2,1,0:T(8,128)} %get-tuple-element.287) | copy-start | bytes 12582916 | tf_op jit(solution)/shard_map/while
  332.1 14.2 %copy-start = (f32[1,8,64,2048]{3,2,1,0:T(8,128)S(1)}, f32[1,8,64,2048]{3,2,1,0:T(8,128)}, u32[]{:S(2)}) copy-start(f32[1,8,64,2048]{3,2,1,0:T(8,128)} %get-tuple-element.288) | copy-start | bytes 12582916 | tf_op jit(solution)/shard_map/while
  332.1 14.2 %copy-start.1 = (f32[1,8,64,2048]{3,2,1,0:T(8,128)S(1)}, f32[1,8,64,2048]{3,2,1,0:T(8,128)}, u32[]{:S(2)}) copy-start(f32[1,8,64,2048]{3,2,1,0:T(8,128)} %get-tuple-element.287) | copy-start | bytes 12582916 | tf_op jit(solution)/shard_map/while
  390.3 14.3 %copy-start = (f32[1,8,64,2048]{3,2,1,0:T(8,128)S(1)}, f32[1,8,64,2048]{3,2,1,0:T(8,128)}, u32[]{:S(2)}) copy-start(f32[1,8,64,2048]{3,2,1,0:T(8,128)} %get-tuple-element.288) | copy-start | bytes 12582916 | tf_op jit(solution)/shard_map/while
  390.3 14.3 %copy-start.1 = (f32[1,8,64,2048]{3,2,1,0:T(8,128)S(1)}, f32[1,8,64,2048]{3,2,1,0:T(8,128)}, u32[]{:S(2)}) copy-start(f32[1,8,64,2048]{3,2,1,0:T(8,128)} %get-tuple-element.287) | copy-start | bytes 12582916 | tf_op jit(solution)/shard_map/while
  411.7 15.6 %collective-permute-start.4 = (f32[1,4,64,256]{3,2,1,0:T(8,128)}, f32[1,4,64,256]{3,2,1,0:T(8,128)S(1)}, u32[]{:S(2)}, u32[]{:S(2)}) collective-permute-start(f32[1,4,64,256]{3,2,1,0:T(8,128)} %get-tuple-element.204), channel_id=1, source_target_pairs={{0,16},{16,0},{32,48},{48,32},{64,80},{80,64},{96,112},{112,96},{1... | collective-permute-start | bytes 786440 | tf_op jit(solution)/shard_map/ppermute | solution.py:31
  417.1 13.9 %collective-permute-start.5 = (f32[1,4,64,256]{3,2,1,0:T(8,128)}, f32[1,4,64,256]{3,2,1,0:T(8,128)S(1)}, u32[]{:S(2)}, u32[]{:S(2)}) collective-permute-start(f32[1,4,64,256]{3,2,1,0:T(8,128)} %get-tuple-element.203), channel_id=1, source_target_pairs={{0,32},{16,48},{32,0},{48,16},{64,96},{80,112},{96,64},{112,80},{1... | collective-permute-start | bytes 786440 | tf_op jit(solution)/shard_map/ppermute | solution.py:31
  423.7 12.6 %collective-permute-start.6 = (f32[1,4,64,256]{3,2,1,0:T(8,128)}, f32[1,4,64,256]{3,2,1,0:T(8,128)S(1)}, u32[]{:S(2)}, u32[]{:S(2)}) collective-permute-start(f32[1,4,64,256]{3,2,1,0:T(8,128)} %get-tuple-element.202), channel_id=1, source_target_pairs={{0,48},{16,32},{32,16},{48,0},{64,112},{80,96},{96,80},{112,64},{1... | collective-permute-start | bytes 786440 | tf_op jit(solution)/shard_map/ppermute | solution.py:31
  423.9 20.1 %collective-permute-start.7 = (f32[1,4,64,256]{3,2,1,0:T(8,128)S(1)}, f32[1,4,64,256]{3,2,1,0:T(8,128)S(1)}, u32[]{:S(2)}, u32[]{:S(2)}) collective-permute-start(f32[1,4,64,256]{3,2,1,0:T(8,128)S(1)} %get-tuple-element.201), channel_id=1, source_target_pairs={{0,64},{16,80},{32,96},{48,112},{64,0},{80,16},{96,32},{112,48},{1... | collective-permute-start | bytes 786440 | tf_op jit(solution)/shard_map/ppermute | solution.py:31
  427.3 22.0 %collective-permute-start.8 = (f32[1,4,64,256]{3,2,1,0:T(8,128)S(1)}, f32[1,4,64,256]{3,2,1,0:T(8,128)S(1)}, u32[]{:S(2)}, u32[]{:S(2)}) collective-permute-start(f32[1,4,64,256]{3,2,1,0:T(8,128)S(1)} %get-tuple-element.200), channel_id=1, source_target_pairs={{0,80},{16,64},{32,112},{48,96},{64,16},{80,0},{96,48},{112,32},{1... | collective-permute-start | bytes 786440 | tf_op jit(solution)/shard_map/ppermute | solution.py:31
  427.3 22.0 %collective-permute-start.9 = (f32[1,4,64,256]{3,2,1,0:T(8,128)S(1)}, f32[1,4,64,256]{3,2,1,0:T(8,128)S(1)}, u32[]{:S(2)}, u32[]{:S(2)}) collective-permute-start(f32[1,4,64,256]{3,2,1,0:T(8,128)S(1)} %get-tuple-element.199), channel_id=1, source_target_pairs={{0,96},{16,112},{32,64},{48,80},{64,32},{80,48},{96,0},{112,16},{1... | collective-permute-start | bytes 786440 | tf_op jit(solution)/shard_map/ppermute | solution.py:31
  431.1 22.1 %collective-permute-start.10 = (f32[1,4,64,256]{3,2,1,0:T(8,128)S(1)}, f32[1,4,64,256]{3,2,1,0:T(8,128)S(1)}, u32[]{:S(2)}, u32[]{:S(2)}) collective-permute-start(f32[1,4,64,256]{3,2,1,0:T(8,128)S(1)} %get-tuple-element.198), channel_id=1, source_target_pairs={{0,112},{16,96},{32,80},{48,64},{64,48},{80,32},{96,16},{112,0},{1... | collective-permute-start | bytes 786440 | tf_op jit(solution)/shard_map/ppermute | solution.py:31
  453.2 1.3 copy-start.3
